TPU v7x, 512 devices: a whole 4x8x8 slice. The times are simulated.
512 devices in a mesh: space: 32 (over z, x), brow: 8 (over y), bcol: 2 (over core).
Axes of the slice: x: 4, y: 8, z: 8, core: 2. Of those that a mesh axis runs over, the one named last changes fastest.
Arguments:
- orbitals: float32 [589824, 256], P(('space', 'brow'), 'bcol'), may hold values from -0.0078125 to 0.0078125
- applied: float32 [589824, 256], P(('space', 'brow'), 'bcol'), may hold values from -0.0078125 to 0.0078125
- cotangent: float32 [589824, 256], P(('space', 'brow'), 'bcol'), may hold values from -6 to 6
- rotation: float32 [256, 256], P('brow', 'bcol'), may hold values from -0.5 to 1.5, as said below
- levels: float32 [256], replicated, may hold values from -3 to 9.8, as said below
Outputs:
- orbital_grad: float32 [589824, 256], P(('space', 'brow'), 'bcol')
Inputs may be any that keep to these rules, and one draw needn't show every extreme that they name: rotation has a unit diagonal plus independent entries of deviation 0.4 / sqrt(256). levels rise with the index, neighbours at least 0.025 apart.
All inputs are finite; a program needn't handle non-finite values.
Results may differ from a plain program's by a relative error of at most 0.0003.
Values sent between devices are 32-bit elements; how exact they have to be, the bound alone decides.
No kernel may reach another device: no remote copies, remote signals or barrier semaphores. Data moves between devices by JAX's collectives and lax.ppermute only.
A program may use at most 64 MiB of HBM per device.

v0:
```python
import jax
import jax.numpy as jnp
from jax import lax
from jax.sharding import PartitionSpec as P


def matmul(left, right):
    return jnp.dot(left, right, preferred_element_type=jnp.float32, precision=lax.Precision.HIGHEST)


def inner_cells(left, right):
    return lax.dot_general(
        left,
        right,
        (((0,), (0,)), ((), ())),
        preferred_element_type=jnp.float32,
        precision=lax.Precision.HIGHEST,
    )


def outer_bands(left, right):
    return lax.dot_general(
        left,
        right,
        (((1,), (1,)), ((), ())),
        preferred_element_type=jnp.float32,
        precision=lax.Precision.HIGHEST,
    )


def subspace(rotation, levels, grad_rot):
    gram_rot = inner_cells(rotation, grad_rot)
    level_gaps = levels[None, :] - levels[:, None]
    diag_mask = jnp.eye(levels.shape[0], dtype=bool)
    inverse = jnp.where(
        diag_mask, jnp.float32(0.0), 1.0 / jnp.where(diag_mask, jnp.float32(1.0), level_gaps)
    )
    mixing = inverse * gram_rot
    sym_ham = mixing + mixing.T
    sym_ovl = mixing * levels[None, :] + levels[:, None] * mixing.T + jnp.diag(jnp.diag(gram_rot))
    ham_coef = outer_bands(matmul(rotation, sym_ham), rotation)
    ovl_coef = -outer_bands(matmul(rotation, sym_ovl), rotation)
    return (ham_coef, ovl_coef)


def band_plan(orbitals, applied, cotangent, row_panel, levels):
    band_width = orbitals.shape[1]
    band_first = lax.axis_index("bcol") * band_width
    orb_whole = lax.all_gather(orbitals, "bcol", axis=1, tiled=True)
    col_sums = lax.psum(inner_cells(orb_whole, cotangent), ("space", "brow"))
    grad_rot, full_rot = (
        lax.all_gather(col_sums, "bcol", axis=1, tiled=True),
        lax.all_gather(row_panel, "bcol", axis=1, tiled=True),
    )
    ham_coef, ovl_coef = subspace(full_rot, levels, grad_rot)
    app_whole, cot_whole = (
        lax.all_gather(applied, "bcol", axis=1, tiled=True),
        lax.all_gather(cotangent, "bcol", axis=1, tiled=True),
    )
    ovl_cols = lax.dynamic_slice_in_dim(ovl_coef, band_first, band_width, 1)
    ham_cols = lax.dynamic_slice_in_dim(ham_coef, band_first, band_width, 1)
    rot_rows = lax.dynamic_slice_in_dim(full_rot, band_first, band_width, 0)
    result = (
        matmul(orb_whole, ovl_cols) + matmul(app_whole, ham_cols) + outer_bands(cot_whole, rot_rows)
    )
    return result


def body(orbitals, applied, cotangent, rotation, levels):
    row_panel = lax.all_gather(rotation, "brow", axis=0, tiled=True)
    result = band_plan(orbitals, applied, cotangent, row_panel, levels)
    return result


def solution(mesh):
    return jax.shard_map(
        body,
        mesh=mesh,
        in_specs=(
            P(("space", "brow"), "bcol"),
            P(("space", "brow"), "bcol"),
            P(("space", "brow"), "bcol"),
            P("brow", "bcol"),
            P(),
        ),
        out_specs=P(("space", "brow"), "bcol"),
        check_vma=False,
    )
```

profile of v0, /device:TPU:1, one launch (start us, length us, event | category | flops | bytes accessed | tf_op | source)
XLA Modules:
  0.0 323.9 jit_solution(460007272820262635)
XLA Ops:
  6.5 0.7 all-gather.4.cloned.1.call-update
  7.3 27.9 %all-gather.4.cloned.1.call-done = f32[2304,256]{1,0:T(8,128)} async-done(((f32[2304,128]{1,0:T(8,128)}), f32[2304,256]{1,0:T(8,128)}) %all-gather.4.cloned.1.call-update) | async-done | bytes 2359312 | tf_op jit(solution)/shard_map/all_gather | solution.py:49
  35.2 6.1 %fusion.20 = f32[256,128]{1,0:T(8,128)} fusion(f32[2304,256]{1,0:T(8,128)} %all-gather.4.cloned.1.call-done, f32[2304,128]{1,0:T(8,128)S(1)} %copy-done.1), kind=kOutput, calls=%fused_computation.29 | convolution fusion | flops 905969664 | bytes 3670016 | tf_op jit(solution)/shard_map/dot_general | solution.py:12
  41.4 0.0 all-gather.6.cloned.1.call-start
  41.4 0.7 all-gather.6.cloned.1.call-update
  42.2 0.5 all-gather.8.cloned.1.call-update
  42.7 18.6 %all_gather.20 = f32[256,128]{1,0:T(8,128)S(1)} all-gather(f32[32,128]{1,0:T(8,128)S(1)} %copy-done.2), channel_id=1, replica_groups=mesh['space'=32,'brow'=8,'bcol'=2] {'brow'}, dimensions={0}, use_global_device_ids=true | all-gather | bytes 147456 | tf_op jit(solution)/shard_map/all_gather | solution.py:70
  61.4 7.9 %all_gather.21 = f32[256,256]{1,0:T(8,128)S(1)} all-gather(f32[256,128]{1,0:T(8,128)S(1)} %all_gather.20), channel_id=1, replica_groups=mesh['space'=32,'brow'=8,'bcol'=2] {'bcol'}, dimensions={1}, use_global_device_ids=true | all-gather | bytes 393216 | tf_op jit(solution)/shard_map/all_gather | solution.py:53
  69.2 197.0 %all-reduce.2.cloned.1.call-done = f32[256,128]{1,0:T(8,128)} async-done(((f32[256,128]{1,0:T(8,128)}), f32[256,128]{1,0:T(8,128)}) %all-reduce.2.cloned.1.call-update) | async-done | bytes 131088 | tf_op jit(solution)/shard_map/psum | solution.py:50
  266.3 7.2 %all_gather.19 = f32[256,256]{1,0:T(8,128)S(1)} all-gather(f32[256,128]{1,0:T(8,128)} %all-reduce.2.cloned.1.call-done), channel_id=1, replica_groups=mesh['space'=32,'brow'=8,'bcol'=2] {'bcol'}, dimensions={1}, use_global_device_ids=true | all-gather | bytes 393216 | tf_op jit(solution)/shard_map/all_gather | solution.py:52
  273.5 0.6 fusion.21
  274.1 0.1 copy.8
  274.2 2.3 gather_fusion
  276.6 0.7 fusion.3
  277.3 0.6 fusion.22
  277.9 0.7 fusion.1
  278.6 0.6 fusion.23
  279.2 0.3 copy-done
  279.6 2.6 fusion.9
  282.2 7.3 %all-gather.6.cloned.1.call-done = f32[2304,256]{1,0:T(8,128)} async-done(((f32[2304,128]{1,0:T(8,128)}), f32[2304,256]{1,0:T(8,128)}) %all-gather.6.cloned.1.call-update) | async-done | bytes 2359312 | tf_op jit(solution)/shard_map/all_gather | solution.py:57
  289.5 4.3 %convolution_add_fusion.1 = f32[128,2304]{1,0:T(8,128)S(1)} fusion(f32[128,2304]{1,0:T(8,128)S(1)} %fusion.9, f32[2304,256]{1,0:T(8,128)} %all-gather.6.cloned.1.call-done, f32[256,256]{1,0:T(8,128)S(1)} %fusion.23, s32[]{:T(128)S(6)} %select_n.34), kind=kOutput, calls=%fused_computation.2 | convolution fusion | flops 906264576 | bytes 4849668 | tf_op jit(solution)/shard_map/dot_general | solution.py:8
  293.8 18.0 %all-gather.8.cloned.1.call-done = f32[2304,256]{1,0:T(8,128)} async-done(((f32[2304,128]{1,0:T(8,128)}), f32[2304,256]{1,0:T(8,128)}) %all-gather.8.cloned.1.call-update) | async-done | bytes 2359312 | tf_op jit(solution)/shard_map/all_gather | solution.py:58
  311.8 4.2 %fusion = f32[2304,128]{0,1:T(8,128)S(1)} fusion(f32[128,2304]{1,0:T(8,128)S(1)} %convolution_add_fusion.1, f32[2304,256]{1,0:T(8,128)} %all-gather.8.cloned.1.call-done, f32[256,256]{1,0:T(8,128)S(1)} %all_gather.21, s32[]{:T(128)S(6)} %select_n.34), kind=kOutput, calls=%fused_computation.3 | convolution fusion | flops 906264576 | bytes 4849668 | tf_op jit(solution)/shard_map/dot_general | solution.py:22
  316.0 1.4 copy.9
  (12 shorter events, 0.1 us)
Async XLA Ops:
  6.5 28.7 %copy-start.1 = (f32[2304,128]{1,0:T(8,128)S(1)}, f32[2304,128]{1,0:T(8,128)}, u32[]{:S(2)}) copy-start(f32[2304,128]{1,0:T(8,128)} %param.7) | copy-start | bytes 3538948
  6.5 28.7 %all-gather.4.cloned.1.call-start = ((), (), s32[]{:S(2)}) async-start(), calls=%async_computation | async-start | bytes 3538944 | tf_op jit(solution)/shard_map/all_gather | solution.py:49
  7.3 259.0 %all-reduce.2.cloned.1.call-start = ((), (), s32[]{:S(2)}) async-start(), calls=%async_computation.1 | async-start | bytes 262144 | tf_op jit(solution)/shard_map/psum | solution.py:50
  41.4 1.3 copy-start.2
  41.4 248.1 %all-gather.6.cloned.1.call-start = ((), (), s32[]{:S(2)}) async-start(), calls=%async_computation.2 | async-start | bytes 3538944 | tf_op jit(solution)/shard_map/all_gather | solution.py:57
  42.1 269.6 %all-gather.8.cloned.1.call-start = ((), (), s32[]{:S(2)}) async-start(), calls=%async_computation.3 | async-start | bytes 3538944 | tf_op jit(solution)/shard_map/all_gather | solution.py:58
  273.5 3.1 copy-start.3
  277.9 1.7 copy-start
Sparse Core Ops, SparseCore 0:
  9.4 25.7 all-gather.3
  41.5 224.7 all-reduce.1
  268.5 20.8 all-gather.5
  291.6 20.1 all-gather.7
where the time goes:
time: 324 us
  waiting for transfers between devices  252 us (78%)
  blocking collectives  33.7 us (10%)
  matrix products  20.4 us (6%)
  between operations  13.2 us (4%)
  local copies, waits for them, and re-layouts  4.21 us (1%)
    psum x1, waiting for transfers between devices, band_plan(): col_sums = lax.psum(inner_cells(orb_whole, cotangent), ('space', 'brow'))  197 us
    all_gather x1, waiting for transfers between devices, band_plan(): orb_whole = lax.all_gather(orbitals, 'bcol', axis=1, tiled=True)  27.9 us
    all_gather x1, blocking collectives, body(): row_panel = lax.all_gather(rotation, 'brow', axis=0, tiled=True)  18.6 us
    all_gather x1, waiting for transfers between devices, band_plan(): lax.all_gather(cotangent, 'bcol', axis=1, tiled=True)  18 us
    dot_general x4, matrix products, matmul(): jnp.dot(left, right, preferred_element_type=jnp.float32, precision=lax.Pr...  8.33 us
    all_gather x1, blocking collectives, band_plan(): lax.all_gather(row_panel, 'bcol', axis=1, tiled=True)  7.88 us
    all_gather x1, waiting for transfers between devices, band_plan(): lax.all_gather(applied, 'bcol', axis=1, tiled=True)  7.28 us
    all_gather x1, blocking collectives, band_plan(): lax.all_gather(col_sums, 'bcol', axis=1, tiled=True)  7.22 us
  transfers between devices with their start and end apart: 4, of which 4 were waited for; matrix products, arithmetic and copies ran while one was open for 4% of the time, Pallas kernels for 0%

commit v1 on v0

--- a/solution.py
+++ b/solution.py
@@ -47,7 +47,9 @@
     band_width = orbitals.shape[1]
     band_first = lax.axis_index("bcol") * band_width
     orb_whole = lax.all_gather(orbitals, "bcol", axis=1, tiled=True)
-    col_sums = lax.psum(inner_cells(orb_whole, cotangent), ("space", "brow"))
+    x = inner_cells(orb_whole, cotangent)
+    shards = lax.all_gather(x, ("space", "brow"), axis=0, tiled=False)
+    col_sums = shards.sum(axis=0)
     grad_rot, full_rot = (
         lax.all_gather(col_sums, "bcol", axis=1, tiled=True),
         lax.all_gather(row_panel, "bcol", axis=1, tiled=True),

time: 324 us -> 314 us (0.969)
  waiting for transfers between devices: 252 us -> 234 us
  other arithmetic: 0.01 us -> 12.2 us
  blocking collectives: 33.7 us -> 29.4 us
    psum x1 -> x0, waiting for transfers between devices: 197 us -> none  [band_plan(): col_sums = lax.psum(inner_cells(orb_whole, cotangent), ('space', 'brow'))]
    all_gather x0 -> x1, waiting for transfers between devices: none -> 190 us  [band_plan(): shards = lax.all_gather(x, ('space', 'brow'), axis=0, tiled=False)]
    reduce_sum x0 -> x1, other arithmetic: none -> 12.2 us  [band_plan(): col_sums = shards.sum(axis=0)]
    all_gather x1, waiting for transfers between devices: 7.28 us -> 0.02 us  [band_plan(): lax.all_gather(applied, 'bcol', axis=1, tiled=True)]
    all_gather x1, blocking collectives: 7.22 us -> 2.89 us  [band_plan(): lax.all_gather(col_sums, 'bcol', axis=1, tiled=True)]
    all_gather x1, waiting for transfers between devices: 18 us -> 14.3 us  [band_plan(): lax.all_gather(cotangent, 'bcol', axis=1, tiled=True)]
  transfers between devices with their start and end apart: 4 -> 4, of which waited for: 4 -> 3; matrix products, arithmetic and copies ran while one was open for 4% -> 8% of each run, Pallas kernels for 0% -> 0%
where the time goes in v1:
time: 314 us
  waiting for transfers between devices  234 us (75%)
  blocking collectives  29.4 us (9%)
  matrix products  20.5 us (7%)
  between operations  13.2 us (4%)
  other arithmetic  12.2 us (4%)
  local copies, waits for them, and re-layouts  4.21 us (1%)
    all_gather x1, waiting for transfers between devices, band_plan(): shards = lax.all_gather(x, ('space', 'brow'), axis=0, tiled=False)  190 us
    all_gather x1, waiting for transfers between devices, band_plan(): orb_whole = lax.all_gather(orbitals, 'bcol', axis=1, tiled=True)  27.9 us
    all_gather x1, blocking collectives, body(): row_panel = lax.all_gather(rotation, 'brow', axis=0, tiled=True)  18.6 us
    all_gather x1, waiting for transfers between devices, band_plan(): lax.all_gather(cotangent, 'bcol', axis=1, tiled=True)  14.3 us
    reduce_sum x1, other arithmetic, band_plan(): col_sums = shards.sum(axis=0)  12.2 us
    dot_general x4, matrix products, matmul(): jnp.dot(left, right, preferred_element_type=jnp.float32, precision=lax.Pr...  8.34 us
    all_gather x1, blocking collectives, band_plan(): lax.all_gather(row_panel, 'bcol', axis=1, tiled=True)  7.86 us
    dot_general x2, matrix products, inner_cells(): lax.dot_general(left, right, (((0,), (0,)), ((), ())), preferred_element_...  6.74 us
  transfers between devices with their start and end apart: 4, of which 3 were waited for; matrix products, arithmetic and copies ran while one was open for 8% of the time, Pallas kernels for 0%

profile of v1, /device:TPU:1, one launch (start us, length us, event | category | flops | bytes accessed | tf_op | source)
XLA Modules:
  0.0 313.6 jit_solution(12135250595857794140)
XLA Ops:
  6.5 0.7 all-gather.6.cloned.1.call-update
  7.3 27.9 %all-gather.6.cloned.1.call-done = f32[2304,256]{1,0:T(8,128)} async-done(((f32[2304,128]{1,0:T(8,128)}), f32[2304,256]{1,0:T(8,128)}) %all-gather.6.cloned.1.call-update) | async-done | bytes 2359312 | tf_op jit(solution)/shard_map/all_gather | solution.py:49
  35.2 6.1 %fusion.20 = f32[256,128]{1,0:T(8,128)} fusion(f32[2304,256]{1,0:T(8,128)} %all-gather.6.cloned.1.call-done, f32[2304,128]{1,0:T(8,128)S(1)} %copy-done.1), kind=kOutput, calls=%fused_computation.29 | convolution fusion | flops 905969664 | bytes 3670016 | tf_op jit(solution)/shard_map/dot_general | solution.py:12
  41.4 0.0 all-gather.8.cloned.1.call-start
  41.4 0.7 all-gather.8.cloned.1.call-update
  42.2 0.5 all-gather.10.cloned.1.call-update
  42.7 18.6 %all_gather.28 = f32[256,128]{1,0:T(8,128)S(1)} all-gather(f32[32,128]{1,0:T(8,128)S(1)} %copy-done.2), channel_id=1, replica_groups=mesh['space'=32,'brow'=8,'bcol'=2] {'brow'}, dimensions={0}, use_global_device_ids=true | all-gather | bytes 147456 | tf_op jit(solution)/shard_map/all_gather | solution.py:72
  61.4 7.9 %all_gather.29 = f32[256,256]{1,0:T(8,128)S(1)} all-gather(f32[256,128]{1,0:T(8,128)S(1)} %all_gather.28), channel_id=1, replica_groups=mesh['space'=32,'brow'=8,'bcol'=2] {'bcol'}, dimensions={1}, use_global_device_ids=true | all-gather | bytes 393216 | tf_op jit(solution)/shard_map/all_gather | solution.py:55
  69.2 189.8 %all-gather.12.cloned.1.call-done = f32[65536,128]{1,0:T(8,128)} async-done(((f32[256,128]{1,0:T(8,128)}), f32[65536,128]{1,0:T(8,128)}) %all-gather.12.cloned.1.call-update) | async-done | bytes 33554448 | tf_op jit(solution)/shard_map/all_gather | solution.py:51
  259.0 12.2 %reduce_sum.9 = f32[256,128]{1,0:T(8,128)S(1)} reduce(f32[256,256,128]{2,1,0:T(8,128)} %bitcast.25, f32[]{:T(128)} %constant.7.clone.1), dimensions={0}, to_apply=%region_0.0 | reduce | flops 8355840 | bytes 33685508 | tf_op jit(solution)/shard_map/reduce_sum | solution.py:52
  271.2 2.9 all_gather.27
  274.1 0.6 fusion.21
  274.7 0.1 copy.8
  274.9 2.3 gather_fusion
  277.2 0.7 fusion.3
  278.0 0.6 fusion.22
  278.6 0.7 fusion.1
  279.3 0.6 fusion.23
  279.9 0.3 copy-done
  280.2 2.6 fusion.9
  282.9 4.3 %convolution_add_fusion.1 = f32[128,2304]{1,0:T(8,128)S(1)} fusion(f32[128,2304]{1,0:T(8,128)S(1)} %fusion.9, f32[2304,256]{1,0:T(8,128)} %all-gather.8.cloned.1.call-done, f32[256,256]{1,0:T(8,128)S(1)} %fusion.23, s32[]{:T(128)S(6)} %select_n.34), kind=kOutput, calls=%fused_computation.2 | convolution fusion | flops 906264576 | bytes 4849668 | tf_op jit(solution)/shard_map/dot_general | solution.py:8
  287.2 14.3 %all-gather.10.cloned.1.call-done = f32[2304,256]{1,0:T(8,128)} async-done(((f32[2304,128]{1,0:T(8,128)}), f32[2304,256]{1,0:T(8,128)}) %all-gather.10.cloned.1.call-update) | async-done | bytes 2359312 | tf_op jit(solution)/shard_map/all_gather | solution.py:60
  301.5 4.2 %fusion = f32[2304,128]{0,1:T(8,128)S(1)} fusion(f32[128,2304]{1,0:T(8,128)S(1)} %convolution_add_fusion.1, f32[2304,256]{1,0:T(8,128)} %all-gather.10.cloned.1.call-done, f32[256,256]{1,0:T(8,128)S(1)} %all_gather.29, s32[]{:T(128)S(6)} %select_n.34), kind=kOutput, calls=%fused_computation.3 | convolution fusion | flops 906264576 | bytes 4849668 | tf_op jit(solution)/shard_map/dot_general | solution.py:22
  305.6 1.4 copy.9
  (13 shorter events, 0.1 us)
Async XLA Ops:
  6.5 28.7 %copy-start.1 = (f32[2304,128]{1,0:T(8,128)S(1)}, f32[2304,128]{1,0:T(8,128)}, u32[]{:S(2)}) copy-start(f32[2304,128]{1,0:T(8,128)} %param.7) | copy-start | bytes 3538948
  6.5 28.7 %all-gather.6.cloned.1.call-start = ((), (), s32[]{:S(2)}) async-start(), calls=%async_computation | async-start | bytes 3538944 | tf_op jit(solution)/shard_map/all_gather | solution.py:49
  7.3 251.8 %all-gather.12.cloned.1.call-start = ((), (), s32[]{:S(2)}) async-start(), calls=%async_computation.3 | async-start | bytes 33685504 | tf_op jit(solution)/shard_map/all_gather | solution.py:51
  41.4 1.3 copy-start.2
  41.4 241.5 %all-gather.8.cloned.1.call-start = ((), (), s32[]{:S(2)}) async-start(), calls=%async_computation.1 | async-start | bytes 3538944 | tf_op jit(solution)/shard_map/all_gather | solution.py:59
  42.1 259.3 %all-gather.10.cloned.1.call-start = ((), (), s32[]{:S(2)}) async-start(), calls=%async_computation.2 | async-start | bytes 3538944 | tf_op jit(solution)/shard_map/all_gather | solution.py:60
  274.1 3.1 copy-start.3
  278.6 1.7 copy-start
Sparse Core Ops, SparseCore 0:
  9.4 25.7 all-gather.5
  41.5 217.4 all-gather.11
  261.1 18.2 all-gather.7
  281.3 20.1 all-gather.9
